TPU v7x, 32 devices: a whole 2x2x4 slice. The times are simulated.
32 devices in a mesh: expert: 4 (over x, core), latent: 8 (over z, y).
Axes of the slice: x: 2, y: 2, z: 4, core: 2. Of those that a mesh axis runs over, the one named last changes fastest.
Arguments:
- tokens: bfloat16 [256, 2560], P(('expert', 'latent')), may hold values from -6 to 6
- route: int32 [256, 1], P(('expert', 'latent')), may hold values from 0 to 3; in each aligned block of 8 rows (0 to 7, 8 to 15, ...) at most 2 rows name the same one
- blocks: int32 [256, 64], P(('expert', 'latent')), may hold values from 0 to 63, all different within a row
- weight: bfloat16 [4, 2560, 8192], P('expert', None, 'latent'), may hold values from -0.125 to 0.125
- enc_bias: float32 [4, 8192], P('expert', 'latent'), may hold values from -3 to 3
- dec_bias: float32 [2560], replicated, may hold values from -3 to 3
Outputs:
- grad_weight: bfloat16 [4, 2560, 8192], P('expert', None, 'latent')
- grad_enc: float32 [4, 8192], P('expert', 'latent')
- grad_dec: float32 [2560], replicated
- loss: float32 [], replicated
Inputs may be any that keep to these rules, and one draw needn't show every extreme that they name: `route`: within the rows of one device (aligned blocks of 8 rows) no expert is named by more than 2 rows. Each row lists 64 different blocks.
All inputs are finite; a program needn't handle non-finite values.
Results may differ from a plain program's by a relative error of at most 0.012.
The roundings to bfloat16 on the way count: a program that leaves them out, or rounds other values in their place, can miss the bound.
Values may be sent and summed in bfloat16 or wider, within the bound.
A program may use at most 128 MiB of HBM per device.

v0:
```python
import jax
import jax.numpy as jnp
from jax import lax
from jax.sharding import PartitionSpec as P

BLK = 128
CAP = 2


def shards(tokens, route, blocks, weight, enc_bias, dec_bias):
    n_expert = lax.axis_size("expert")
    n_latent = lax.axis_size("latent")
    width = tokens.shape[1]
    list_len = blocks.shape[1]
    expert_of = route[:, 0]
    one_hot = (expert_of[:, None] == jnp.arange(n_expert, dtype=jnp.int32)[None, :]).astype(
        jnp.int32
    )
    earlier = jnp.sum((jnp.cumsum(one_hot, axis=0) - one_hot) * one_hot, axis=1)
    target = expert_of * CAP + earlier
    send_rows = jnp.zeros((n_expert * CAP, width), jnp.bfloat16).at[target].set(tokens)
    send_rows = send_rows.reshape(n_expert, CAP, width)
    send_lists = jnp.full((n_expert * CAP, list_len), -1, jnp.int32).at[target].set(blocks)
    send_lists = send_lists.reshape(n_expert, CAP, list_len)
    got_rows, got_lists = (
        lax.all_to_all(send_rows, "expert", split_axis=0, concat_axis=0, tiled=True),
        lax.all_to_all(send_lists, "expert", split_axis=0, concat_axis=0, tiled=True),
    )
    all_rows, all_lists = (
        lax.all_gather(got_rows[None], "latent", axis=0, tiled=True),
        lax.all_gather(got_lists[None], "latent", axis=0, tiled=True),
    )
    token_rows = all_rows.reshape(-1, width)
    listed = all_lists.reshape(-1, list_len)
    row_count = token_rows.shape[0]
    valid = (listed[:, 0] >= 0).astype(jnp.float32)
    slice_index = lax.axis_index("latent")
    weights_here = weight[0]
    per_slice = weights_here.shape[1] // BLK
    own_blocks = slice_index * per_slice + jnp.arange(per_slice, dtype=jnp.int32)
    chosen = jnp.any(listed[:, :, None] == own_blocks[None, None, :], axis=1).astype(jnp.float32)
    mask = jnp.repeat(chosen, BLK, axis=1)
    rows_f32 = token_rows.astype(jnp.float32)
    shifted = (rows_f32 - dec_bias).astype(jnp.bfloat16)
    pre_act = jnp.dot(shifted, weights_here, preferred_element_type=jnp.float32) + enc_bias[0]
    active = jnp.maximum(pre_act, 0.0) * mask
    active_bf = active.astype(jnp.bfloat16)
    share = row_count // n_latent
    first_row = slice_index * share
    along_width = (((1,), (1,)), ((), ()))
    partial_sum = lax.dot_general(
        active_bf, weights_here, along_width, preferred_element_type=jnp.float32
    )
    summed = lax.psum(partial_sum, "latent")
    error_all = (summed + dec_bias - rows_f32) * valid[:, None]
    error_bf = error_all.astype(jnp.bfloat16)
    error_share = lax.dynamic_slice_in_dim(error_all, first_row, share, 0)
    grad_act = jnp.dot(error_bf, weights_here, preferred_element_type=jnp.float32)
    grad_pre = grad_act * (pre_act > 0.0).astype(jnp.float32) * mask
    grad_pre_bf = grad_pre.astype(jnp.bfloat16)
    along_rows = (((0,), (0,)), ((), ()))
    grad_here = lax.dot_general(
        shifted, grad_pre_bf, along_rows, preferred_element_type=jnp.float32
    )
    grad_here = grad_here + lax.dot_general(
        error_bf, active_bf, along_rows, preferred_element_type=jnp.float32
    )
    grad_bias = jnp.sum(grad_pre, axis=0)
    pulled = jnp.dot(
        weights_here, grad_bias.astype(jnp.bfloat16), preferred_element_type=jnp.float32
    )
    bias_term = jnp.sum(error_share, axis=0) - pulled
    loss_term = 0.5 * jnp.sum(error_share * error_share)
    grad_dec, loss_sum = lax.psum((bias_term, loss_term), ("expert", "latent"))
    loss = loss_sum / (tokens.shape[0] * n_expert * n_latent)
    return (grad_here.astype(jnp.bfloat16)[None], grad_bias[None], grad_dec, loss)


def solution(mesh):
    return jax.shard_map(
        shards,
        mesh=mesh,
        in_specs=(
            P(("expert", "latent"), None),
            P(("expert", "latent"), None),
            P(("expert", "latent"), None),
            P("expert", None, "latent"),
            P("expert", "latent"),
            P(),
        ),
        out_specs=(P("expert", None, "latent"), P("expert", "latent"), P(), P()),
        check_vma=False,
    )
```

profile of v0, /device:TPU:0, one launch (start us, length us, event | category | flops | bytes accessed | tf_op | source)
XLA Modules:
  0.0 231.5 jit_solution(9575406962594364959)
XLA Ops:
  7.2 0.7 fusion.31
  8.0 0.7 select_reduce_fusion
  8.7 0.7 fusion.32
  9.3 0.7 scatter_custom_fusion.1
  10.1 0.7 reshape.68
  10.8 4.2 %all-to-all-start.1 = ((s32[4,1,128]{2,1,0:T(1,128)}), s32[4,1,128]{2,1,0:T(1,128)S(1)}, u32[]{:S(2)}, u32[]{:S(2)}) async-start(s32[4,1,128]{2,1,0:T(1,128)} %reshape.68), calls=%async_computation.1 | async-start | bytes 4096 | tf_op jit(solution)/shard_map/all_to_all | solution.py:27
  15.0 0.9 scatter_custom_fusion
  15.9 0.6 reshape.33
  16.5 2.1 all-to-all-done.1
  18.6 3.3 %all-to-all-start = ((bf16[4,2,2560]{2,1,0:T(2,128)(2,1)}), bf16[4,2,2560]{2,1,0:T(2,128)(2,1)S(1)}, u32[]{:S(2)}, u32[]{:S(2)}) async-start(bf16[4,2,2560]{2,1,0:T(2,128)(2,1)} %reshape.33), calls=%async_computation | async-start | bytes 81920 | tf_op jit(solution)/shard_map/all_to_all | solution.py:26
  22.5 0.7 reduce.4
  23.2 31.2 %all-gather.1 = s32[32,2,64]{2,1,0:T(2,128)S(1)} all-gather(s32[4,2,64]{2,1,0:T(2,128)S(1)} %reshape.69), channel_id=3, replica_groups=mesh['expert'=4,'latent'=8] {'latent'}, dimensions={0}, use_global_device_ids=true | all-gather | bytes 18432 | tf_op jit(solution)/shard_map/all_gather | solution.py:31
  54.4 1.2 compare_reduce_fusion
  55.7 30.9 %all-gather = bf16[32,2,2560]{2,1,0:T(2,128)(2,1)S(1)} all-gather(bf16[4,2,2560]{2,1,0:T(2,128)(2,1)S(1)} %all-to-all-done), channel_id=2, replica_groups=mesh['expert'=4,'latent'=8] {'latent'}, dimensions={0}, use_global_device_ids=true | all-gather | bytes 368640 | tf_op jit(solution)/shard_map/all_gather | solution.py:30
  86.8 0.9 subtract_convert_fusion
  88.0 3.7 %fusion.23 = (bf16[64,1024]{1,0:T(8,128)(2,1)S(1)}, f32[64,1024]{1,0:T(8,128)S(1)}) fusion(f32[8,8,8,128]{3,2,1,0:T(8,128)S(1)} %bitcast.49, f32[1024]{0:T(1024)} %bitcast.55, bf16[64,2560]{1,0:T(8,128)(2,1)S(1)} %convert_element_type.47, bf16[1,2560,1024]{2,1,0:T(8,128)(2,1)} %param.9), kind=kOutput, calls=%fused_computation.22 | convolution fusion | flops 335806464 | bytes 6230016 | tf_op jit(solution)/shard_map/dot_general | solution.py:45
  91.9 2.5 %fusion.4 = f32[64,2560]{1,0:T(8,128)} fusion(bf16[64,1024]{1,0:T(8,128)(2,1)S(1)} %get-tuple-element.8, bf16[1,2560,1024]{2,1,0:T(8,128)(2,1)S(1)} %copy-done), kind=kOutput, calls=%fused_computation.7 | convolution fusion | flops 335544320 | bytes 6029312 | tf_op jit(solution)/shard_map/dot_general | solution.py:51
  94.7 74.7 %all-reduce.3.cloned.1.call-done = f32[64,2560]{1,0:T(8,128)} async-done(((f32[64,2560]{1,0:T(8,128)}), f32[64,2560]{1,0:T(8,128)}) %all-reduce.3.cloned.1.call-update) | async-done | bytes 655376 | tf_op jit(solution)/shard_map/psum | solution.py:54
  169.3 1.3 subtract_multiply_fusion
  170.6 3.7 %fusion.33 = (f32[1024]{0:T(1024)S(1)}, bf16[64,1024]{1,0:T(8,128)(2,1)S(1)}) fusion(f32[8,8,8,128]{3,2,1,0:T(8,128)S(1)} %bitcast.50, bf16[1,2560,1024]{2,1,0:T(8,128)(2,1)} %param.9, f32[64,2560]{1,0:T(8,128)S(1)} %subtract_multiply_fusion, f32[64,1024]{1,0:T(8,128)S(1)} %get-tuple-element.9), kind=kOutput, calls=%fused_computation.42 | convolution fusion | flops 336034816 | bytes 6557696 | tf_op jit(solution)/shard_map/dot_general | solution.py:58
  174.4 1.6 fusion.21
  175.9 3.9 %fusion.8 = bf16[1,2560,1024]{2,1,0:T(8,128)(2,1)} fusion(f32[2560,1024]{1,0:T(8,128)S(1)} %fusion.21, bf16[64,1024]{1,0:T(8,128)(2,1)S(1)} %get-tuple-element.8, f32[64,2560]{1,0:T(8,128)S(1)} %subtract_multiply_fusion), kind=kOutput, calls=%fused_computation.11 | convolution fusion | flops 340951040 | bytes 16515072 | tf_op jit(solution)/shard_map/dot_general | solution.py:65
  179.9 1.5 fusion.18
  182.7 40.2 %all-reduce = (f32[2560]{0:T(1024)}, f32[]{:T(128)}) all-reduce(f32[2560]{0:T(1024)S(1)} %sub.28, f32[]{:T(128)S(6)} %mul_shard_map.3), channel_id=1, replica_groups=mesh['expert'=4,'latent'=8] {'expert','latent'}, use_global_device_ids=true, to_apply=%region_8.9 | all-reduce | flops 2561 | bytes 20488 | tf_op jit(solution)/shard_map/psum | solution.py:74
  (28 shorter events, 2.4 us)
Async XLA Ops:
  10.8 7.9 %all-to-all-start.1 = ((s32[4,1,128]{2,1,0:T(1,128)}), s32[4,1,128]{2,1,0:T(1,128)S(1)}, u32[]{:S(2)}, u32[]{:S(2)}) async-start(s32[4,1,128]{2,1,0:T(1,128)} %reshape.68), calls=%async_computation.1 | async-start | bytes 4096 | tf_op jit(solution)/shard_map/all_to_all | solution.py:27
  18.6 37.0 %all-to-all-start = ((bf16[4,2,2560]{2,1,0:T(2,128)(2,1)}), bf16[4,2,2560]{2,1,0:T(2,128)(2,1)S(1)}, u32[]{:S(2)}, u32[]{:S(2)}) async-start(bf16[4,2,2560]{2,1,0:T(2,128)(2,1)} %reshape.33), calls=%async_computation | async-start | bytes 81920 | tf_op jit(solution)/shard_map/all_to_all | solution.py:26
  21.9 147.4 %all-reduce.3.cloned.1.call-start = ((), (), s32[]{:S(2)}) async-start(), calls=%async_computation.2 | async-start | bytes 1310720 | tf_op jit(solution)/shard_map/psum | solution.py:54
  87.8 4.1 %copy-start = (bf16[1,2560,1024]{2,1,0:T(8,128)(2,1)S(1)}, bf16[1,2560,1024]{2,1,0:T(8,128)(2,1)}, u32[]{:S(2)}) copy-start(bf16[1,2560,1024]{2,1,0:T(8,128)(2,1)} %param.9) | copy-start | bytes 15728644
  91.7 77.7 %copy-start.1 = (f32[2560]{0:T(1024)S(1)}, f32[2560]{0:T(1024)}, u32[]{:S(2)}) copy-start(f32[2560]{0:T(1024)} %param.11) | copy-start | bytes 30724
  170.6 9.3 %slice-start = ((s8[5242880]{0:T(1024)(128)(4,1)}), s8[4194304]{0:T(1024)(128)(4,1)S(1)}, s32[]{:S(2)}) async-start(s8[5242880]{0:T(1024)(128)(4,1)} %bitcast.46), calls=%async_computation.3 | async-start | bytes 8388608
  174.4 5.5 %copy-start.2 = (f32[1024]{0:T(1024)}, f32[1024]{0:T(1024)S(1)}, u32[]{:S(2)}) copy-start(f32[1024]{0:T(1024)S(1)} %get-tuple-element.10) | copy-start | bytes 12292
  174.4 5.5 %slice-start.1 = ((s8[5242880]{0:T(1024)(128)(4,1)}), s8[1048576]{0:T(1024)(128)(4,1)S(1)}, s32[]{:S(2)}) async-start(s8[5242880]{0:T(1024)(128)(4,1)} %bitcast.46), calls=%async_computation.4 | async-start | bytes 2097152
Sparse Core Ops, SparseCore 0:
  94.6 74.7 all-reduce.2
where the time goes:
time: 232 us; the launch traced here: 231 us
  blocking collectives  102 us (44%)
  waiting for transfers between devices  76.8 us (33%)
  matrix products  16.9 us (7%)
  between operations  16.6 us (7%)
  starting transfers between devices  7.52 us (3%)
  other arithmetic  7.25 us (3%)
  local copies, waits for them, and re-layouts  4.12 us (2%)
    psum x1, waiting for transfers between devices, shards(): summed = lax.psum(partial_sum, 'latent')  74.7 us
    psum x1, blocking collectives, shards(): grad_dec, loss_sum = lax.psum((bias_term, loss_term), ('expert', 'latent'))  40.2 us
    all_gather x1, blocking collectives, shards(): lax.all_gather(got_lists[None], 'latent', axis=0, tiled=True)  31.2 us
    all_gather x1, blocking collectives, shards(): lax.all_gather(got_rows[None], 'latent', axis=0, tiled=True)  30.9 us
  transfers between devices with their start and end apart: 3, of which 2 were waited for; matrix products, arithmetic and copies ran while one was open for 2% of the time, Pallas kernels for 0%

commit v1 on v0

v1 whole, which is shorter than its diff:
```python
import functools
import jax
import jax.numpy as jnp
from jax import lax
from jax.experimental import pallas as pl
from jax.experimental.pallas import tpu as pltpu
from jax.sharding import PartitionSpec as P

BLK = 128
CAP = 2
PACK = 16
PARTS = PACK // CAP
LANES = 128
TILE = 256
MESH = pl.DeviceIdType.MESH
ALONG_LAST = (((1,), (1,)), ((), ()))
ALONG_FIRST = (((0,), (0,)), ((), ()))


def step_kernel(
    n_e, n_l, n_tok, width, list_len,
    tok_ref, route_ref, blocks_ref, w_hbm, encb_ref, decb_ref,
    left_ref, right_ref, genc_ref, gdec_ref, loss_ref,
    w_ref, aug, pack, mine, gathered, rows, shifted, gate, part, rs_send, rs_recv, ag_recv, err, vec_e, vec_l,
    w_sem, s1, r1, s2, r2, s3, r3, s4, r4, s5, r5, s6, r6,
):
    me_e = lax.axis_index("expert")
    me_l = lax.axis_index("latent")
    share = n_e * CAP
    count = n_l * share
    half = width // 2
    chunk = aug.shape[1] // PARTS
    latents = w_ref.shape[1]

    def to_expert(src, dst, ssem, rsem, peer, slot):
        return pltpu.make_async_remote_copy(
            src_ref=src, dst_ref=dst, send_sem=ssem.at[peer], recv_sem=rsem.at[slot],
            device_id=(peer, me_l), device_id_type=MESH)

    def to_latent(src, dst, ssem, rsem, peer, slot):
        return pltpu.make_async_remote_copy(
            src_ref=src, dst_ref=dst, send_sem=ssem.at[peer], recv_sem=rsem.at[slot],
            device_id=(me_e, peer), device_id_type=MESH)

    def peers(me, n):
        return [lax.rem(me + k, n) for k in range(1, n)]

    w_copy = pltpu.make_async_copy(w_hbm.at[0], w_ref, w_sem)
    w_copy.start()
    barrier = pltpu.get_barrier_semaphore()
    for p in peers(me_e, n_e):
        pl.semaphore_signal(barrier, inc=1, device_id=(p, me_l), device_id_type=MESH)
    for p in peers(me_l, n_l):
        pl.semaphore_signal(barrier, inc=1, device_id=(me_e, p), device_id_type=MESH)

    aug[...] = jnp.zeros_like(aug)
    aug[:, :width] = tok_ref[...].astype(jnp.float32)
    aug[:, width:width + list_len] = (blocks_ref[...] + 1).astype(jnp.float32)
    route = route_ref[...]
    one_hot = (route == lax.broadcasted_iota(jnp.int32, (n_tok, LANES), 1)).astype(jnp.float32)
    before = (lax.broadcasted_iota(jnp.int32, (n_tok, n_tok), 1)
              < lax.broadcasted_iota(jnp.int32, (n_tok, n_tok), 0)).astype(jnp.float32)
    earlier = jnp.sum(jnp.dot(before, one_hot, preferred_element_type=jnp.float32) * one_hot, axis=1, keepdims=True)
    target = route.astype(jnp.float32) * CAP + earlier
    target = jnp.concatenate([target] * PARTS, axis=0)
    stacked = jnp.concatenate([aug[:, c * chunk:(c + 1) * chunk] for c in range(PARTS)], axis=0).astype(jnp.bfloat16)
    shape = (PARTS * n_tok, n_e * PACK)
    row = lax.broadcasted_iota(jnp.int32, shape, 0)
    col = lax.broadcasted_iota(jnp.int32, shape, 1)
    place = (col >> 4) * CAP + (col & 1)
    hit = (target == place.astype(jnp.float32)) & ((row >> 3) == ((col >> 1) & (PARTS - 1)))
    packed = lax.dot_general(hit.astype(jnp.bfloat16), stacked, ALONG_FIRST, preferred_element_type=jnp.float32)
    pack[...] = packed.astype(jnp.bfloat16).reshape(pack.shape)

    pl.semaphore_wait(barrier, (n_e - 1) + (n_l - 1))
    for p in peers(me_e, n_e):
        to_expert(pack.at[p], mine.at[me_e], s1, r1, p, me_e).start()
    mine[me_e] = pack[me_e]
    for p in peers(me_e, n_e):
        to_expert(pack.at[p], mine.at[p], s1, r1, p, p).wait_recv()
    for p in peers(me_l, n_l):
        to_latent(mine, gathered.at[me_l], s2, r2, p, me_l).start()

    shape = (n_e * PACK, n_e * PACK)
    row = lax.broadcasted_iota(jnp.int32, shape, 0)
    col = lax.broadcasted_iota(jnp.int32, shape, 1)
    unpack = (row == ((col >> 1) & (PARTS - 1)) * share + (col >> 4) * CAP + (col & 1)).astype(jnp.bfloat16)

    def place_rows(source, block):
        flat = jnp.dot(unpack, block.reshape(n_e * PACK, chunk), preferred_element_type=jnp.float32)
        at = pl.ds(pl.multiple_of(source * share, 8), share)
        for c in range(rows.shape[1] // chunk):
            rows[at, c * chunk:(c + 1) * chunk] = flat[c * share:(c + 1) * share]

    place_rows(me_l, mine[...])

    @pl.loop(1, n_l)
    def _(k):
        p = lax.rem(me_l + k, n_l)
        to_latent(mine, gathered.at[p], s2, r2, p, p).wait_recv()
        place_rows(p, gathered[p])

    decb = decb_ref[...]
    bf = (rows[:, :width] - decb).astype(jnp.bfloat16)
    shifted[...] = bf
    left_ref[:count, :] = bf
    lists = rows[:, width:width + LANES]
    first_block = me_l * (latents // BLK)
    for b in range(latents // BLK):
        number = (first_block + b + 1).astype(jnp.float32)
        found = jnp.max((lists == number).astype(jnp.float32), axis=1, keepdims=True)
        gate[:, b * BLK:(b + 1) * BLK] = jnp.broadcast_to(found, (count, BLK))

    w_copy.wait()

    @pl.loop(0, latents // TILE)
    def _(j):
        at = pl.ds(pl.multiple_of(j * TILE, TILE), TILE)
        pre = jnp.dot(shifted[...], w_ref[:, at], preferred_element_type=jnp.float32) + encb_ref[:, at]
        mask = gate[:, at]
        right_ref[count:, at] = (jnp.maximum(pre, 0.0) * mask).astype(jnp.bfloat16)
        gate[:, at] = jnp.where(pre > 0.0, mask, 0.0)

    @pl.loop(0, width // TILE)
    def _(j):
        at = pl.ds(pl.multiple_of(j * TILE, TILE), TILE)
        part[:, at] = lax.dot_general(
            right_ref[count:, :], w_ref[at, :], ALONG_LAST, preferred_element_type=jnp.float32)

    def folded(value):
        return jnp.concatenate([value[:, :half], value[:, half:]], axis=0)

    @pl.loop(1, n_l)
    def _(k):
        p = lax.rem(me_l + k, n_l)
        rs_send[p] = folded(part[pl.ds(pl.multiple_of(p * share, 8), share), :]).astype(jnp.bfloat16)
        to_latent(rs_send.at[p], rs_recv.at[me_l], s3, r3, p, me_l).start()

    own = pl.ds(pl.multiple_of(me_l * share, 8), share)
    rs_recv[me_l] = folded(part[own, :]).astype(jnp.bfloat16)
    for p in peers(me_l, n_l):
        to_latent(rs_send.at[p], rs_recv.at[p], s3, r3, p, p).wait_recv()
    total = jnp.zeros((2 * share, half), jnp.float32)
    for s in range(n_l):
        total = total + rs_recv[s].astype(jnp.float32)
    recon = jnp.concatenate([total[:share], total[share:]], axis=1) + decb
    valid = (rows[own, width:width + 1] > 0.5).astype(jnp.float32)
    error = (recon - rows[own, :width]) * valid
    ag_recv[me_l] = folded(error).astype(jnp.bfloat16)
    for p in peers(me_l, n_l):
        to_latent(ag_recv.at[me_l], ag_recv.at[me_l], s4, r4, p, me_l).start()
    error_sum = jnp.sum(error, axis=0, keepdims=True)
    loss = 0.5 * jnp.sum(error * error)
    for p in peers(me_l, n_l):
        to_latent(ag_recv.at[p], ag_recv.at[p], s4, r4, p, p).wait_recv()

    @pl.loop(0, n_l)
    def _(s):
        got = ag_recv[s].astype(jnp.float32)
        at = pl.ds(pl.multiple_of(s * share, 8), share)
        err[at, :half] = got[:share]
        err[at, half:] = got[share:]

    left_ref[count:, :] = err[...].astype(jnp.bfloat16)

    @pl.loop(0, latents // TILE)
    def _(j):
        at = pl.ds(pl.multiple_of(j * TILE, TILE), TILE)
        grad = jnp.dot(left_ref[count:, :], w_ref[:, at], preferred_element_type=jnp.float32) * gate[:, at]
        right_ref[:count, at] = grad.astype(jnp.bfloat16)
        genc_ref[:, at] = jnp.sum(grad, axis=0, keepdims=True)

    column = jnp.broadcast_to(genc_ref[...], (8, latents)).astype(jnp.bfloat16)
    for j in range(width // TILE):
        at = slice(j * TILE, (j + 1) * TILE)
        pulled = lax.dot_general(column, w_ref[at, :], ALONG_LAST, preferred_element_type=jnp.float32)
        vec_e[me_e, :, at] = error_sum[:, at] - pulled[:1]
    vec_e[me_e, :, width:] = jnp.broadcast_to(loss.reshape(1, 1), (1, LANES))

    for p in peers(me_e, n_e):
        to_expert(vec_e.at[me_e], vec_e.at[me_e], s5, r5, p, me_e).start()
    for p in peers(me_e, n_e):
        to_expert(vec_e.at[p], vec_e.at[p], s5, r5, p, p).wait_recv()
    vec = vec_e[0]
    for s in range(1, n_e):
        vec = vec + vec_e[s]
    vec_l[me_l] = vec
    for p in peers(me_l, n_l):
        to_latent(vec_l.at[me_l], vec_l.at[me_l], s6, r6, p, me_l).start()
    for p in peers(me_l, n_l):
        to_latent(vec_l.at[p], vec_l.at[p], s6, r6, p, p).wait_recv()
    vec = vec_l[0]
    for s in range(1, n_l):
        vec = vec + vec_l[s]
    gdec_ref[...] = vec[:, :width]
    loss_ref[...] = vec[:, width:] * (1.0 / (n_tok * n_e * n_l))

    for p in peers(me_e, n_e):
        to_expert(pack.at[p], mine.at[me_e], s1, r1, p, me_e).wait_send()
        to_expert(vec_e.at[me_e], vec_e.at[me_e], s5, r5, p, me_e).wait_send()
    for p in peers(me_l, n_l):
        to_latent(mine, gathered.at[me_l], s2, r2, p, me_l).wait_send()
        to_latent(rs_send.at[p], rs_recv.at[me_l], s3, r3, p, me_l).wait_send()
        to_latent(ag_recv.at[me_l], ag_recv.at[me_l], s4, r4, p, me_l).wait_send()
        to_latent(vec_l.at[me_l], vec_l.at[me_l], s6, r6, p, me_l).wait_send()


def shards(tokens, route, blocks, weight, enc_bias, dec_bias):
    n_e = lax.axis_size("expert")
    n_l = lax.axis_size("latent")
    n_tok, width = tokens.shape
    list_len = blocks.shape[1]
    latents = weight.shape[2]
    share = n_e * CAP
    count = n_l * share
    aug_width = -(-(width + LANES) // (PARTS * LANES)) * PARTS * LANES
    chunk = aug_width // PARTS
    row_width = -(-(width + LANES) // chunk) * chunk
    vmem = pl.BlockSpec(memory_space=pltpu.VMEM)
    dma = pltpu.SemaphoreType.DMA
    f32, bf16 = jnp.float32, jnp.bfloat16
    left, right, genc, gdec, loss = pl.pallas_call(
        functools.partial(step_kernel, n_e, n_l, n_tok, width, list_len),
        out_shape=(
            jax.ShapeDtypeStruct((2 * count, width), bf16),
            jax.ShapeDtypeStruct((2 * count, latents), bf16),
            jax.ShapeDtypeStruct((1, latents), f32),
            jax.ShapeDtypeStruct((1, width), f32),
            jax.ShapeDtypeStruct((1, LANES), f32),
        ),
        in_specs=[vmem, vmem, vmem, pl.BlockSpec(memory_space=pl.ANY), vmem, vmem],
        out_specs=[vmem] * 5,
        scratch_shapes=[
            pltpu.VMEM((width, latents), bf16),
            pltpu.VMEM((n_tok, aug_width), f32),
            pltpu.VMEM((n_e, PACK, chunk), bf16),
            pltpu.VMEM((n_e, PACK, chunk), bf16),
            pltpu.VMEM((n_l, n_e, PACK, chunk), bf16),
            pltpu.VMEM((count, row_width), f32),
            pltpu.VMEM((count, width), bf16),
            pltpu.VMEM((count, latents), f32),
            pltpu.VMEM((count, width), f32),
            pltpu.VMEM((n_l, 2 * share, width // 2), bf16),
            pltpu.VMEM((n_l, 2 * share, width // 2), bf16),
            pltpu.VMEM((n_l, 2 * share, width // 2), bf16),
            pltpu.VMEM((count, width), f32),
            pltpu.VMEM((n_e, 1, width + LANES), f32),
            pltpu.VMEM((n_l, 1, width + LANES), f32),
            dma,
            dma((n_e,)), dma((n_e,)),
            dma((n_l,)), dma((n_l,)),
            dma((n_l,)), dma((n_l,)),
            dma((n_l,)), dma((n_l,)),
            dma((n_e,)), dma((n_e,)),
            dma((n_l,)), dma((n_l,)),
        ],
        compiler_params=pltpu.CompilerParams(
            collective_id=0, has_side_effects=True, vmem_limit_bytes=56 << 20),
        name="sae_step",
    )(tokens, route, blocks, weight, enc_bias, dec_bias[None])
    grad = lax.dot_general(left, right, ALONG_FIRST, preferred_element_type=f32)
    return grad.astype(bf16)[None], genc, gdec[0], loss[0, 0]


def solution(mesh):
    return jax.shard_map(
        shards,
        mesh=mesh,
        in_specs=(
            P(("expert", "latent"), None),
            P(("expert", "latent"), None),
            P(("expert", "latent"), None),
            P("expert", None, "latent"),
            P("expert", "latent"),
            P(),
        ),
        out_specs=(P("expert", None, "latent"), P("expert", "latent"), P(), P()),
        check_vma=False,
    )
```

time: 232 us -> 64.1 us (0.28)
  blocking collectives: 102 us -> 0 us
  waiting for transfers between devices: 76.8 us -> 0 us
  Pallas kernels: 0 us -> 52.8 us
  between operations: 16.6 us -> 1.83 us
  matrix products: 16.9 us -> 5.06 us
  starting transfers between devices: 7.52 us -> 0 us
  other arithmetic: 7.25 us -> 0.63 us
    psum x1 -> x0, waiting for transfers between devices: 74.7 us -> none  [shards(): summed = lax.psum(partial_sum, 'latent')]
    all_gather x2 -> x0, blocking collectives: 62 us -> none  [the longest x1 31.2 us: shards(): lax.all_gather(got_lists[None], 'latent', axis=0, tiled=True)]
    pallas_call x0 -> x1, Pallas kernels: none -> 52.8 us  [shards(): pl.pallas_call(functools.partial(step_kernel, n_e, n_l, n_tok, width, lis...]
    psum x1 -> x0, blocking collectives: 40.2 us -> none  [shards(): grad_dec, loss_sum = lax.psum((bias_term, loss_term), ('expert', 'latent'))]
    dot_general x6 -> x1, matrix products: 16.9 us -> 5.06 us  [shards(): grad = lax.dot_general(left, right, ALONG_FIRST, preferred_element_type=f32)]
    all_to_all x2 -> x0, starting transfers between devices: 7.48 us -> none  [the longest x1 4.21 us: shards(): lax.all_to_all(send_lists, 'expert', split_axis=0, concat_axis=0, tiled=T...]
  transfers between devices with their start and end apart: 3 -> 0, of which waited for: 2 -> 0; matrix products, arithmetic and copies ran while one was open for 2% -> 0% of each run, Pallas kernels for 0% -> 0%
where the time goes in v1:
time: 64.1 us; the launch traced here: 63.6 us
  Pallas kernels  52.8 us (82%)
  matrix products  5.06 us (8%)
  local copies, waits for them, and re-layouts  3.24 us (5%)
  between operations  1.83 us (3%)
    pallas_call x1, Pallas kernels, shards(): pl.pallas_call(functools.partial(step_kernel, n_e, n_l, n_tok, width, lis...  52.8 us
    dot_general x1, matrix products, shards(): grad = lax.dot_general(left, right, ALONG_FIRST, preferred_element_type=f32)  5.06 us
    unnamed x8, local copies, waits for them, and re-layouts  1.93 us
    broadcast_in_dim x1, local copies, waits for them, and re-layouts, shards(): dec_bias[None]  1.31 us

profile of v1, /device:TPU:0, one launch (start us, length us, event | category | flops | bytes accessed | tf_op | source)
XLA Modules:
  0.0 63.6 jit_solution(17457839875561371370)
XLA Ops:
  0.6 1.3 %broadcast_in_dim.6.decb_ref = f32[1,2560]{1,0:T(1,128)} reshape(f32[2560]{0:T(1024)} %param.11) | data formatting | bytes 20480 | tf_op jit(solution)/shard_map/broadcast_in_dim | solution.py:260
  1.9 1.3 %copy.10.route_ref = s32[8,1]{1,0:T(8,128)} copy(s32[8,1]{0,1:T(1,128)} %param.7) | data formatting | bytes 64 | tf_op args[1]
  3.3 52.8 %sae_step.1 = (bf16[128,2560]{1,0:T(8,128)(2,1)}, bf16[128,1024]{1,0:T(8,128)(2,1)}, f32[1,1024]{1,0:T(1,128)}, f32[1,2560]{1,0:T(1,128)}, f32[1,128]{1,0:T(1,128)}) custom-call(bf16[8,2560]{1,0:T(8,128)(2,1)} %tok_ref.1, s32[8,1]{1,0:T(8,128)} %copy.10.route_ref, s32[8,64]{1,0:T(8,128)} %blocks_ref.1, bf16[1,2560,1024]{2,1,0:T(8,128)(2,1)} %w_hbm.1, ...), custom_call_target="tpu_custom_call" | custom-call | tf_op jit(solution)/shard_map/sae_step/pallas_call | solution.py:222
  56.1 0.0 copy-start
  56.1 0.0 copy-start.1
  56.1 0.0 copy-start.2
  56.1 5.1 %fusion = bf16[1,2560,1024]{2,1,0:T(8,128)(2,1)} fusion(bf16[128,2560]{1,0:T(8,128)(2,1)} %get-tuple-element.9, bf16[128,1024]{1,0:T(8,128)(2,1)} %get-tuple-element.10), kind=kOutput, calls=%fused_computation.1 | convolution fusion | flops 673710080 | bytes 6160384 | tf_op jit(solution)/shard_map/dot_general | solution.py:261
  61.2 0.0 copy-done
  61.2 0.6 reduce
  61.8 0.0 copy-done.1
  61.8 0.6 copy.13
  62.4 0.0 copy-done.2
Async XLA Ops:
  56.1 5.1 %copy-start = (f32[1,2560]{1,0:T(1,128)S(1)}, f32[1,2560]{1,0:T(1,128)}, u32[]{:S(2)}) copy-start(f32[1,2560]{1,0:T(1,128)} %get-tuple-element.12) | copy-start | bytes 30724
  56.1 5.7 %copy-start.1 = (f32[1,1024]{1,0:T(1,128)S(1)}, f32[1,1024]{1,0:T(1,128)}, u32[]{:S(2)}) copy-start(f32[1,1024]{1,0:T(1,128)} %get-tuple-element.19) | copy-start | bytes 12292
  56.1 6.3 %copy-start.2 = (f32[1,128]{1,0:T(1,128)S(1)}, f32[1,128]{1,0:T(1,128)}, u32[]{:S(2)}) copy-start(f32[1,128]{1,0:T(1,128)} %get-tuple-element.13) | copy-start | bytes 1540

commit v2 on v1

v2 whole, which is shorter than its diff:
```python
import functools
import jax
import jax.numpy as jnp
from jax import lax
from jax.experimental import pallas as pl
from jax.experimental.pallas import tpu as pltpu
from jax.sharding import PartitionSpec as P

BLK = 128
CAP = 2
PACK = 16
PARTS = PACK // CAP
LANES = 128
TILE = 256
MESH = pl.DeviceIdType.MESH
ALONG_LAST = (((1,), (1,)), ((), ()))
ALONG_FIRST = (((0,), (0,)), ((), ()))


def step_kernel(
    n_e, n_l, n_tok, width, list_len,
    tok_ref, route_ref, blocks_ref, w_hbm, encb_ref, decb_ref,
    left_ref, right_ref, genc_ref, gdec_ref, loss_ref,
    w_ref, aug, pack, mine, gathered, rows, shifted, gate, part, rs_send, rs_recv, ag_recv, err, acc, vec_e, vec_l,
    w_sem, s1, r1, s2, r2, s3, r3, s4, r4, s5, r5, s6, r6,
):
    me_e = lax.axis_index("expert")
    me_l = lax.axis_index("latent")
    share = n_e * CAP
    count = n_l * share
    half = width // 2
    quarter = half // 2
    chunk = aug.shape[1] // PARTS
    latents = w_ref.shape[1]

    def to_expert(src, dst, ssem, rsem, peer, slot):
        return pltpu.make_async_remote_copy(
            src_ref=src, dst_ref=dst, send_sem=ssem.at[peer], recv_sem=rsem.at[slot],
            device_id=(peer, me_l), device_id_type=MESH)

    def to_latent(src, dst, ssem, rsem, peer, slot):
        return pltpu.make_async_remote_copy(
            src_ref=src, dst_ref=dst, send_sem=ssem.at[peer], recv_sem=rsem.at[slot],
            device_id=(me_e, peer), device_id_type=MESH)

    def peers(me, n):
        return [lax.rem(me + k, n) for k in range(1, n)]

    partner = me_l + 1 - 2 * lax.rem(me_l, 2)
    alike = [lax.rem(me_l + 2 * k, n_l) for k in range(1, n_l // 2)]

    def spread(src, dst, ssem, rsem):
        for p in alike + [partner]:
            to_latent(src, dst.at[me_l], ssem, rsem, p, me_l).start()

    def collect(dst, ssem, rsem, use):
        @pl.loop(1, n_l // 2)
        def _(k):
            p = lax.rem(me_l + 2 * k, n_l)
            to_latent(dst.at[p], dst.at[p], ssem, rsem, p, p).wait_recv()
            pltpu.make_async_remote_copy(
                src_ref=dst.at[p], dst_ref=dst.at[p], send_sem=ssem.at[n_l + p], recv_sem=rsem.at[p],
                device_id=(me_e, partner), device_id_type=MESH).start()
            use(p)

        @pl.loop(0, n_l // 2)
        def _(k):
            p = lax.rem(partner + 2 * k, n_l)
            to_latent(dst.at[p], dst.at[p], ssem, rsem, p, p).wait_recv()
            use(p)

    def drain(src, dst, ssem, rsem):
        for p in alike + [partner]:
            to_latent(src, dst.at[me_l], ssem, rsem, p, me_l).wait_send()
        for p in alike:
            pltpu.make_async_remote_copy(
                src_ref=dst.at[p], dst_ref=dst.at[p], send_sem=ssem.at[n_l + p], recv_sem=rsem.at[p],
                device_id=(me_e, partner), device_id_type=MESH).wait_send()

    w_copy = pltpu.make_async_copy(w_hbm.at[0], w_ref, w_sem)
    w_copy.start()
    barrier = pltpu.get_barrier_semaphore()
    for p in peers(me_e, n_e):
        pl.semaphore_signal(barrier, inc=1, device_id=(p, me_l), device_id_type=MESH)
    for p in peers(me_l, n_l):
        pl.semaphore_signal(barrier, inc=1, device_id=(me_e, p), device_id_type=MESH)

    aug[...] = jnp.zeros_like(aug)
    aug[:, :width] = tok_ref[...].astype(jnp.float32)
    aug[:, width:width + list_len] = (blocks_ref[...] + 1).astype(jnp.float32)
    route = jnp.broadcast_to(route_ref[...], (8, n_tok))
    one_hot = (route == lax.broadcasted_iota(jnp.int32, (8, n_tok), 0)).astype(jnp.float32)
    before = (lax.broadcasted_iota(jnp.int32, (n_tok, n_tok), 0)
              < lax.broadcasted_iota(jnp.int32, (n_tok, n_tok), 1)).astype(jnp.float32)
    earlier = jnp.sum(jnp.dot(one_hot, before, preferred_element_type=jnp.float32) * one_hot, axis=0, keepdims=True)
    target = (route.astype(jnp.float32) * CAP + earlier).astype(jnp.bfloat16)
    repeat = (lax.broadcasted_iota(jnp.int32, (n_tok, PARTS * n_tok), 0)
              == (lax.broadcasted_iota(jnp.int32, (n_tok, PARTS * n_tok), 1) & (n_tok - 1))).astype(jnp.bfloat16)
    target = jnp.dot(target, repeat, preferred_element_type=jnp.float32)[:1]
    stacked = jnp.concatenate([aug[:, c * chunk:(c + 1) * chunk] for c in range(PARTS)], axis=0).astype(jnp.bfloat16)
    shape = (n_e * PACK, PARTS * n_tok)
    row = lax.broadcasted_iota(jnp.int32, shape, 0)
    col = lax.broadcasted_iota(jnp.int32, shape, 1)
    place = (row >> 4) * CAP + (row & 1)
    hit = (target == place.astype(jnp.float32)) & (col // n_tok == ((row >> 1) & (PARTS - 1)))
    packed = jnp.dot(hit.astype(jnp.bfloat16), stacked, preferred_element_type=jnp.float32)
    pack[...] = packed.astype(jnp.bfloat16).reshape(pack.shape)

    pl.semaphore_wait(barrier, (n_e - 1) + (n_l - 1))
    for p in peers(me_e, n_e):
        to_expert(pack.at[p], mine.at[me_e], s1, r1, p, me_e).start()
    mine[me_e] = pack[me_e]
    for p in peers(me_e, n_e):
        to_expert(pack.at[p], mine.at[p], s1, r1, p, p).wait_recv()
    spread(mine, gathered, s2, r2)

    shape = (n_e * PACK, n_e * PACK)
    row = lax.broadcasted_iota(jnp.int32, shape, 0)
    col = lax.broadcasted_iota(jnp.int32, shape, 1)
    unpack = (row == ((col >> 1) & (PARTS - 1)) * share + (col >> 4) * CAP + (col & 1)).astype(jnp.bfloat16)

    def place_rows(source, block):
        flat = jnp.dot(unpack, block.reshape(n_e * PACK, chunk), preferred_element_type=jnp.float32)
        at = pl.ds(pl.multiple_of(source * share, 8), share)
        for c in range(rows.shape[1] // chunk):
            rows[at, c * chunk:(c + 1) * chunk] = flat[c * share:(c + 1) * share]

    place_rows(me_l, mine[...])

    collect(gathered, s2, r2, lambda p: place_rows(p, gathered[p]))

    decb = decb_ref[...].reshape(1, width)
    bf = (rows[:, :width] - decb).astype(jnp.bfloat16)
    shifted[...] = bf
    left_ref[:count, :] = bf
    lists = rows[:, width:width + LANES]
    first_block = me_l * (latents // BLK)
    for b in range(latents // BLK):
        number = (first_block + b + 1).astype(jnp.float32)
        found = jnp.max((lists == number).astype(jnp.float32), axis=1, keepdims=True)
        gate[:, b * BLK:(b + 1) * BLK] = jnp.broadcast_to(found, (count, BLK))

    w_copy.wait()

    @pl.loop(0, latents // TILE)
    def _(j):
        at = pl.ds(pl.multiple_of(j * TILE, TILE), TILE)
        pre = jnp.dot(shifted[...], w_ref[:, at], preferred_element_type=jnp.float32) + encb_ref[:, at]
        mask = gate[:, at]
        right_ref[count:, at] = (jnp.maximum(pre, 0.0) * mask).astype(jnp.bfloat16)
        gate[:, at] = jnp.where(pre > 0.0, mask, 0.0)

    def folded(value):
        return jnp.concatenate([value[:, :quarter], value[:, quarter:]], axis=0)

    def unfolded(value):
        return jnp.concatenate([value[:share], value[share:]], axis=1)

    own = pl.ds(pl.multiple_of(me_l * share, 8), share)
    for h in range(2):
        @pl.loop(0, half // TILE)
        def _(j):
            at = pl.ds(pl.multiple_of(h * half + j * TILE, TILE), TILE)
            part[:, at] = lax.dot_general(
                right_ref[count:, :], w_ref[at, :], ALONG_LAST, preferred_element_type=jnp.float32)

        cols = slice(h * half, (h + 1) * half)

        @pl.loop(1, n_l)
        def _(k):
            p = lax.rem(me_l + k, n_l)
            rs_send[h, p] = folded(part[pl.ds(pl.multiple_of(p * share, 8), share), cols]).astype(jnp.bfloat16)
            to_latent(rs_send.at[h, p], rs_recv.at[h, me_l], s3.at[h], r3.at[h], p, me_l).start()

    valid = (rows[own, width:width + 1] > 0.5).astype(jnp.float32)
    loss = jnp.zeros((), jnp.float32)
    error_sum = []
    for h in range(2):
        cols = slice(h * half, (h + 1) * half)
        total = part[own, cols]
        for p in peers(me_l, n_l):
            to_latent(rs_send.at[h, p], rs_recv.at[h, p], s3.at[h], r3.at[h], p, p).wait_recv()
            total = total + unfolded(rs_recv[h, p].astype(jnp.float32))
        error = (total + decb[:, cols] - rows[own, cols]) * valid
        ag_recv[h, me_l] = folded(error).astype(jnp.bfloat16)
        spread(ag_recv.at[h, me_l], ag_recv.at[h], s4.at[h], r4.at[h])
        error_sum.append(jnp.sum(error, axis=0, keepdims=True))
        loss = loss + 0.5 * jnp.sum(error * error)
    error_sum = jnp.concatenate(error_sum, axis=1)

    for h in range(2):
        cols = slice(h * half, (h + 1) * half)

        def place_error(s):
            at = pl.ds(pl.multiple_of(s * share, 8), share)
            err[at, :] = unfolded(ag_recv[h, s].astype(jnp.float32))

        place_error(me_l)
        collect(ag_recv.at[h], s4.at[h], r4.at[h], place_error)
        left_ref[count:, cols] = err[...].astype(jnp.bfloat16)

        @pl.loop(0, latents // TILE)
        def _(j):
            at = pl.ds(pl.multiple_of(j * TILE, TILE), TILE)
            grad = jnp.dot(left_ref[count:, cols], w_ref[cols, at], preferred_element_type=jnp.float32)
            if h == 0:
                acc[:, at] = grad
            else:
                grad = (acc[:, at] + grad) * gate[:, at]
                right_ref[:count, at] = grad.astype(jnp.bfloat16)
                genc_ref[:, at] = jnp.sum(grad, axis=0, keepdims=True)

    column = jnp.broadcast_to(genc_ref[...], (8, latents)).astype(jnp.bfloat16)
    for j in range(width // TILE):
        at = slice(j * TILE, (j + 1) * TILE)
        pulled = lax.dot_general(column, w_ref[at, :], ALONG_LAST, preferred_element_type=jnp.float32)
        vec_e[me_e, :, at] = error_sum[:, at] - pulled[:1]
    vec_e[me_e, :, width:] = jnp.broadcast_to(loss.reshape(1, 1), (1, LANES))

    for p in peers(me_e, n_e):
        to_expert(vec_e.at[me_e], vec_e.at[me_e], s5, r5, p, me_e).start()
    for p in peers(me_e, n_e):
        to_expert(vec_e.at[p], vec_e.at[p], s5, r5, p, p).wait_recv()
    vec = vec_e[0]
    for s in range(1, n_e):
        vec = vec + vec_e[s]
    vec_l[me_l] = vec
    for p in peers(me_l, n_l):
        to_latent(vec_l.at[me_l], vec_l.at[me_l], s6, r6, p, me_l).start()
    for p in peers(me_l, n_l):
        to_latent(vec_l.at[p], vec_l.at[p], s6, r6, p, p).wait_recv()
    vec = vec_l[0]
    for s in range(1, n_l):
        vec = vec + vec_l[s]
    gdec_ref[...] = vec[:, :width].reshape(width)
    loss_ref[0] = vec[0, width] * (1.0 / (n_tok * n_e * n_l))

    for p in peers(me_e, n_e):
        to_expert(pack.at[p], mine.at[me_e], s1, r1, p, me_e).wait_send()
        to_expert(vec_e.at[me_e], vec_e.at[me_e], s5, r5, p, me_e).wait_send()
    for p in peers(me_l, n_l):
        to_latent(vec_l.at[me_l], vec_l.at[me_l], s6, r6, p, me_l).wait_send()
    drain(mine, gathered, s2, r2)
    for h in range(2):
        drain(ag_recv.at[h, me_l], ag_recv.at[h], s4.at[h], r4.at[h])
        for p in peers(me_l, n_l):
            to_latent(rs_send.at[h, p], rs_recv.at[h, me_l], s3.at[h], r3.at[h], p, me_l).wait_send()


def grad_kernel(left_ref, right_ref, out_ref):
    out_ref[0] = lax.dot_general(
        left_ref[...], right_ref[...], ALONG_FIRST, preferred_element_type=jnp.float32).astype(out_ref.dtype)


def shards(tokens, route, blocks, weight, enc_bias, dec_bias):
    n_e = lax.axis_size("expert")
    n_l = lax.axis_size("latent")
    n_tok, width = tokens.shape
    list_len = blocks.shape[1]
    latents = weight.shape[2]
    share = n_e * CAP
    count = n_l * share
    aug_width = -(-(width + LANES) // (PARTS * LANES)) * PARTS * LANES
    chunk = aug_width // PARTS
    row_width = -(-(width + LANES) // chunk) * chunk
    vmem = pl.BlockSpec(memory_space=pltpu.VMEM)
    dma = pltpu.SemaphoreType.DMA
    f32, bf16 = jnp.float32, jnp.bfloat16
    left, right, genc, gdec, loss = pl.pallas_call(
        functools.partial(step_kernel, n_e, n_l, n_tok, width, list_len),
        out_shape=(
            jax.ShapeDtypeStruct((2 * count, width), bf16),
            jax.ShapeDtypeStruct((2 * count, latents), bf16),
            jax.ShapeDtypeStruct((1, latents), f32),
            jax.ShapeDtypeStruct((width,), f32),
            jax.ShapeDtypeStruct((1,), f32),
        ),
        in_specs=[vmem, vmem, vmem, pl.BlockSpec(memory_space=pl.ANY), vmem, vmem],
        out_specs=[vmem] * 4 + [pl.BlockSpec(memory_space=pltpu.SMEM)],
        scratch_shapes=[
            pltpu.VMEM((width, latents), bf16),
            pltpu.VMEM((n_tok, aug_width), f32),
            pltpu.VMEM((n_e, PACK, chunk), bf16),
            pltpu.VMEM((n_e, PACK, chunk), bf16),
            pltpu.VMEM((n_l, n_e, PACK, chunk), bf16),
            pltpu.VMEM((count, row_width), f32),
            pltpu.VMEM((count, width), bf16),
            pltpu.VMEM((count, latents), f32),
            pltpu.VMEM((count, width), f32),
            pltpu.VMEM((2, n_l, 2 * share, width // 4), bf16),
            pltpu.VMEM((2, n_l, 2 * share, width // 4), bf16),
            pltpu.VMEM((2, n_l, 2 * share, width // 4), bf16),
            pltpu.VMEM((count, width // 2), f32),
            pltpu.VMEM((count, latents), f32),
            pltpu.VMEM((n_e, 1, width + LANES), f32),
            pltpu.VMEM((n_l, 1, width + LANES), f32),
            dma,
            dma((n_e,)), dma((n_e,)),
            dma((2 * n_l,)), dma((n_l,)),
            dma((2, n_l)), dma((2, n_l)),
            dma((2, 2 * n_l)), dma((2, n_l)),
            dma((n_e,)), dma((n_e,)),
            dma((n_l,)), dma((n_l,)),
        ],
        compiler_params=pltpu.CompilerParams(
            collective_id=0, has_side_effects=True, vmem_limit_bytes=56 << 20),
        name="sae_step",
    )(tokens, route.reshape(1, n_tok), blocks, weight, enc_bias, dec_bias)
    strip = 2 * TILE
    grad = pl.pallas_call(
        grad_kernel,
        out_shape=jax.ShapeDtypeStruct((1, width, latents), bf16),
        grid=(width // strip,),
        in_specs=[
            pl.BlockSpec((2 * count, strip), lambda i: (0, i)),
            pl.BlockSpec((2 * count, latents), lambda i: (0, 0)),
        ],
        out_specs=pl.BlockSpec((1, strip, latents), lambda i: (0, i, 0)),
        compiler_params=pltpu.CompilerParams(vmem_limit_bytes=56 << 20),
        name="grad_weight",
    )(left, right)
    return grad, genc, gdec, loss[0]


def solution(mesh):
    return jax.shard_map(
        shards,
        mesh=mesh,
        in_specs=(
            P(("expert", "latent"), None),
            P(("expert", "latent"), None),
            P(("expert", "latent"), None),
            P("expert", None, "latent"),
            P("expert", "latent"),
            P(),
        ),
        out_specs=(P("expert", None, "latent"), P("expert", "latent"), P(), P()),
        check_vma=False,
    )
```

time: 64.1 us -> 63.1 us (0.984)
  Pallas kernels: 52.8 us -> 59.2 us
  matrix products: 5.06 us -> 0 us
  local copies, waits for them, and re-layouts: 3.24 us -> 1.2 us
    pallas_call x0 -> x1, Pallas kernels: none -> 5.5 us  [shards(): pl.pallas_call(grad_kernel, out_shape=jax.ShapeDtypeStruct((1, width, lat...]
    dot_general x1 -> x0, matrix products: 5.06 us -> none  [shards(): grad = lax.dot_general(left, right, ALONG_FIRST, preferred_element_type=f32)]
    broadcast_in_dim x1 -> x0, local copies, waits for them, and re-layouts: 1.31 us -> none  [shards(): dec_bias[None]]
    pallas_call x1, Pallas kernels: 52.8 us -> 53.7 us  [shards(): pl.pallas_call(functools.partial(step_kernel, n_e, n_l, n_tok, width, lis...]
    unnamed x8 -> x6, local copies, waits for them, and re-layouts: 1.93 us -> 1.2 us
where the time goes in v2:
time: 63.1 us; the launch traced here: 62.8 us
  Pallas kernels  59.2 us (94%)
  between operations  2.34 us (4%)
  local copies, waits for them, and re-layouts  1.2 us (2%)
    pallas_call x1, Pallas kernels, shards(): pl.pallas_call(functools.partial(step_kernel, n_e, n_l, n_tok, width, lis...  53.7 us
    pallas_call x1, Pallas kernels, shards(): pl.pallas_call(grad_kernel, out_shape=jax.ShapeDtypeStruct((1, width, lat...  5.5 us

profile of v2, /device:TPU:0, one launch (start us, length us, event | category | flops | bytes accessed | tf_op | source)
XLA Modules:
  0.0 62.8 jit_solution(5744419689675669013)
XLA Ops:
  0.6 53.7 %sae_step.1 = (bf16[128,2560]{1,0:T(8,128)(2,1)}, bf16[128,1024]{1,0:T(8,128)(2,1)}, f32[1,1024]{1,0:T(1,128)}, f32[2560]{0:T(1024)}, f32[1]{0:T(128)}) custom-call(bf16[8,2560]{1,0:T(8,128)(2,1)} %tok_ref.1, s32[1,8]{1,0:T(1,128)} %bitcast.2, s32[8,64]{1,0:T(8,128)} %blocks_ref.1, bf16[1,2560,1024]{2,1,0:T(8,128)(2,1)} %w_hbm.1, f32[1,1024]{1,0:T(1,128)} %encb_ref.1, ...), custom_call_target="tpu_custom_call" | custom-call | tf_op jit(solution)/shard_map/sae_step/pallas_call | solution.py:269
  54.4 0.0 copy-start.1
  54.4 0.0 copy-start
  54.4 5.5 %grad_weight.1 = bf16[1,2560,1024]{2,1,0:T(8,128)(2,1)} custom-call(bf16[128,2560]{1,0:T(8,128)(2,1)} %get-tuple-element.9.left_ref, bf16[128,1024]{1,0:T(8,128)(2,1)} %get-tuple-element.10.right_ref), custom_call_target="tpu_custom_call" | custom-call | tf_op jit(solution)/shard_map/grad_weight/pallas_call | solution.py:310
  59.9 0.0 copy-done.1
  59.9 0.6 copy.13
  60.5 0.0 copy-done
  60.5 0.6 copy.14
Async XLA Ops:
  54.4 5.5 %copy-start.1 = (f32[1,1024]{1,0:T(1,128)S(1)}, f32[1,1024]{1,0:T(1,128)}, u32[]{:S(2)}) copy-start(f32[1,1024]{1,0:T(1,128)} %get-tuple-element.19) | copy-start | bytes 12292
  54.4 6.1 %copy-start = (f32[2560]{0:T(1024)S(1)}, f32[2560]{0:T(1024)}, u32[]{:S(2)}) copy-start(f32[2560]{0:T(1024)} %get-tuple-element.20) | copy-start | bytes 30724

commit v3 on v2

--- a/solution.py
+++ b/solution.py
@@ -32,6 +32,9 @@
     quarter = half // 2
     chunk = aug.shape[1] // PARTS
     latents = w_ref.shape[1]
+    few = count <= LANES
+    wide = latents if few else TILE
+    deep = half if few else TILE
 
     def to_expert(src, dst, ssem, rsem, peer, slot):
         return pltpu.make_async_remote_copy(
@@ -112,22 +115,24 @@
     mine[me_e] = pack[me_e]
     for p in peers(me_e, n_e):
         to_expert(pack.at[p], mine.at[p], s1, r1, p, p).wait_recv()
-    spread(mine, gathered, s2, r2)
-
     shape = (n_e * PACK, n_e * PACK)
     row = lax.broadcasted_iota(jnp.int32, shape, 0)
     col = lax.broadcasted_iota(jnp.int32, shape, 1)
     unpack = (row == ((col >> 1) & (PARTS - 1)) * share + (col >> 4) * CAP + (col & 1)).astype(jnp.bfloat16)
-
-    def place_rows(source, block):
-        flat = jnp.dot(unpack, block.reshape(n_e * PACK, chunk), preferred_element_type=jnp.float32)
+    flat = jnp.dot(unpack, mine[...].reshape(n_e * PACK, chunk), preferred_element_type=jnp.float32)
+    flat = jnp.concatenate([flat[c * share:(c + 1) * share] for c in range(PARTS)], axis=1)
+    fold = gathered.shape[2]
+    gathered[me_l] = jnp.concatenate([flat[:, :fold], flat[:, fold:2 * fold]], axis=0).astype(jnp.bfloat16)
+    spread(gathered.at[me_l], gathered, s2, r2)
+
+    def place_rows(source):
+        block = gathered[source].astype(jnp.float32)
         at = pl.ds(pl.multiple_of(source * share, 8), share)
-        for c in range(rows.shape[1] // chunk):
-            rows[at, c * chunk:(c + 1) * chunk] = flat[c * share:(c + 1) * share]
-
-    place_rows(me_l, mine[...])
-
-    collect(gathered, s2, r2, lambda p: place_rows(p, gathered[p]))
+        rows[at, :fold] = block[:share]
+        rows[at, fold:] = block[share:]
+
+    place_rows(me_l)
+    collect(gathered, s2, r2, place_rows)
 
     decb = decb_ref[...].reshape(1, width)
     bf = (rows[:, :width] - decb).astype(jnp.bfloat16)
@@ -142,9 +147,9 @@
 
     w_copy.wait()
 
-    @pl.loop(0, latents // TILE)
+    @pl.loop(0, latents // wide)
     def _(j):
-        at = pl.ds(pl.multiple_of(j * TILE, TILE), TILE)
+        at = pl.ds(pl.multiple_of(j * wide, wide), wide)
         pre = jnp.dot(shifted[...], w_ref[:, at], preferred_element_type=jnp.float32) + encb_ref[:, at]
         mask = gate[:, at]
         right_ref[count:, at] = (jnp.maximum(pre, 0.0) * mask).astype(jnp.bfloat16)
@@ -158,9 +163,9 @@
 
     own = pl.ds(pl.multiple_of(me_l * share, 8), share)
     for h in range(2):
-        @pl.loop(0, half // TILE)
+        @pl.loop(0, half // deep)
         def _(j):
-            at = pl.ds(pl.multiple_of(h * half + j * TILE, TILE), TILE)
+            at = pl.ds(pl.multiple_of(h * half + j * deep, deep), deep)
             part[:, at] = lax.dot_general(
                 right_ref[count:, :], w_ref[at, :], ALONG_LAST, preferred_element_type=jnp.float32)
 
@@ -199,9 +204,9 @@
         collect(ag_recv.at[h], s4.at[h], r4.at[h], place_error)
         left_ref[count:, cols] = err[...].astype(jnp.bfloat16)
 
-        @pl.loop(0, latents // TILE)
+        @pl.loop(0, latents // wide)
         def _(j):
-            at = pl.ds(pl.multiple_of(j * TILE, TILE), TILE)
+            at = pl.ds(pl.multiple_of(j * wide, wide), wide)
             grad = jnp.dot(left_ref[count:, cols], w_ref[cols, at], preferred_element_type=jnp.float32)
             if h == 0:
                 acc[:, at] = grad
@@ -240,16 +245,24 @@
         to_expert(vec_e.at[me_e], vec_e.at[me_e], s5, r5, p, me_e).wait_send()
     for p in peers(me_l, n_l):
         to_latent(vec_l.at[me_l], vec_l.at[me_l], s6, r6, p, me_l).wait_send()
-    drain(mine, gathered, s2, r2)
+    drain(gathered.at[me_l], gathered, s2, r2)
     for h in range(2):
         drain(ag_recv.at[h, me_l], ag_recv.at[h], s4.at[h], r4.at[h])
         for p in peers(me_l, n_l):
             to_latent(rs_send.at[h, p], rs_recv.at[h, me_l], s3.at[h], r3.at[h], p, me_l).wait_send()
 
 
-def grad_kernel(left_ref, right_ref, out_ref):
-    out_ref[0] = lax.dot_general(
-        left_ref[...], right_ref[...], ALONG_FIRST, preferred_element_type=jnp.float32).astype(out_ref.dtype)
+def grad_kernel(left_ref, right_ref, genc_in, gdec_in, loss_in, out_ref, genc_out, gdec_out, loss_out):
+    @pl.when(pl.program_id(0) == 0)
+    def _():
+        genc_out[...] = genc_in[...]
+        gdec_out[...] = gdec_in[...]
+        loss_out[0] = loss_in[0]
+
+    for j in range(right_ref.shape[1] // TILE):
+        at = slice(j * TILE, (j + 1) * TILE)
+        out_ref[0, :, at] = lax.dot_general(
+            left_ref[...], right_ref[:, at], ALONG_FIRST, preferred_element_type=jnp.float32).astype(out_ref.dtype)
 
 
 def shards(tokens, route, blocks, weight, enc_bias, dec_bias):
@@ -262,7 +275,7 @@
     count = n_l * share
     aug_width = -(-(width + LANES) // (PARTS * LANES)) * PARTS * LANES
     chunk = aug_width // PARTS
-    row_width = -(-(width + LANES) // chunk) * chunk
+    fold = -(-(width + LANES) // (2 * LANES)) * LANES
     vmem = pl.BlockSpec(memory_space=pltpu.VMEM)
     dma = pltpu.SemaphoreType.DMA
     f32, bf16 = jnp.float32, jnp.bfloat16
@@ -282,8 +295,8 @@
             pltpu.VMEM((n_tok, aug_width), f32),
             pltpu.VMEM((n_e, PACK, chunk), bf16),
             pltpu.VMEM((n_e, PACK, chunk), bf16),
-            pltpu.VMEM((n_l, n_e, PACK, chunk), bf16),
-            pltpu.VMEM((count, row_width), f32),
+            pltpu.VMEM((n_l, 2 * share, fold), bf16),
+            pltpu.VMEM((count, 2 * fold), f32),
             pltpu.VMEM((count, width), bf16),
             pltpu.VMEM((count, latents), f32),
             pltpu.VMEM((count, width), f32),
@@ -306,19 +319,29 @@
             collective_id=0, has_side_effects=True, vmem_limit_bytes=56 << 20),
         name="sae_step",
     )(tokens, route.reshape(1, n_tok), blocks, weight, enc_bias, dec_bias)
-    strip = 2 * TILE
-    grad = pl.pallas_call(
+    strip = TILE
+    small = [
+        pl.BlockSpec((1, latents), lambda i: (0, 0)),
+        pl.BlockSpec((width,), lambda i: (0,)),
+        pl.BlockSpec(memory_space=pltpu.SMEM),
+    ]
+    grad, genc, gdec, loss = pl.pallas_call(
         grad_kernel,
-        out_shape=jax.ShapeDtypeStruct((1, width, latents), bf16),
+        out_shape=(
+            jax.ShapeDtypeStruct((1, width, latents), bf16),
+            jax.ShapeDtypeStruct((1, latents), f32),
+            jax.ShapeDtypeStruct((width,), f32),
+            jax.ShapeDtypeStruct((1,), f32),
+        ),
         grid=(width // strip,),
         in_specs=[
             pl.BlockSpec((2 * count, strip), lambda i: (0, i)),
             pl.BlockSpec((2 * count, latents), lambda i: (0, 0)),
-        ],
-        out_specs=pl.BlockSpec((1, strip, latents), lambda i: (0, i, 0)),
+        ] + small,
+        out_specs=[pl.BlockSpec((1, strip, latents), lambda i: (0, i, 0))] + small,
         compiler_params=pltpu.CompilerParams(vmem_limit_bytes=56 << 20),
         name="grad_weight",
-    )(left, right)
+    )(left, right, genc, gdec, loss)
     return grad, genc, gdec, loss[0]
 
 

time: 63.1 us -> 61.1 us (0.968)
  between operations: 2.34 us -> 0.64 us
  local copies, waits for them, and re-layouts: 1.2 us -> 0 us
    pallas_call x1, Pallas kernels: 5.5 us -> 8.76 us  [shards(): pl.pallas_call(grad_kernel, out_shape=(jax.ShapeDtypeStruct((1, width, la...]
    pallas_call x1, Pallas kernels: 53.7 us -> 51.1 us  [shards(): pl.pallas_call(functools.partial(step_kernel, n_e, n_l, n_tok, width, lis...]
    unnamed x6 -> x0, local copies, waits for them, and re-layouts: 1.2 us -> none
where the time goes in v3:
time: 61.1 us; the launch traced here: 60.5 us
  Pallas kernels  59.8 us (98%)
  between operations  0.64 us (1%)
    pallas_call x1, Pallas kernels, shards(): pl.pallas_call(functools.partial(step_kernel, n_e, n_l, n_tok, width, lis...  51.1 us
    pallas_call x1, Pallas kernels, shards(): pl.pallas_call(grad_kernel, out_shape=(jax.ShapeDtypeStruct((1, width, la...  8.76 us

profile of v3, /device:TPU:0, one launch (start us, length us, event | category | flops | bytes accessed | tf_op | source)
XLA Modules:
  0.0 60.5 jit_solution(13526240884332727082)
XLA Ops:
  0.6 51.1 %sae_step.1 = (bf16[128,2560]{1,0:T(8,128)(2,1)}, bf16[128,1024]{1,0:T(8,128)(2,1)}, f32[1,1024]{1,0:T(1,128)}, f32[2560]{0:T(1024)}, f32[1]{0:T(128)}) custom-call(bf16[8,2560]{1,0:T(8,128)(2,1)} %tok_ref.1, s32[1,8]{1,0:T(1,128)} %bitcast.2, s32[8,64]{1,0:T(8,128)} %blocks_ref.1, bf16[1,2560,1024]{2,1,0:T(8,128)(2,1)} %w_hbm.1, f32[1,1024]{1,0:T(1,128)} %encb_ref.1, ...), custom_call_target="tpu_custom_call" | custom-call | tf_op jit(solution)/shard_map/sae_step/pallas_call | solution.py:282
  51.7 8.8 %grad_weight.1 = (bf16[1,2560,1024]{2,1,0:T(8,128)(2,1)}, f32[1,1024]{1,0:T(1,128)}, f32[2560]{0:T(1024)}, f32[1]{0:T(128)}) custom-call(bf16[128,2560]{1,0:T(8,128)(2,1)} %get-tuple-element.13.left_ref, bf16[128,1024]{1,0:T(8,128)(2,1)} %get-tuple-element.14.right_ref, f32[1,1024]{1,0:T(1,128)} %get-tuple-element.15.genc_in, ...), custom_call_target="tpu_custom_call" | custom-call | tf_op jit(solution)/shard_map/grad_weight/pallas_call | solution.py:328

commit v4 on v3

--- a/solution.py
+++ b/solution.py
@@ -188,7 +188,8 @@
             total = total + unfolded(rs_recv[h, p].astype(jnp.float32))
         error = (total + decb[:, cols] - rows[own, cols]) * valid
         ag_recv[h, me_l] = folded(error).astype(jnp.bfloat16)
-        spread(ag_recv.at[h, me_l], ag_recv.at[h], s4.at[h], r4.at[h])
+        for p in peers(me_l, n_l):
+            to_latent(ag_recv.at[h, me_l], ag_recv.at[h, me_l], s4.at[h], r4.at[h], p, me_l).start()
         error_sum.append(jnp.sum(error, axis=0, keepdims=True))
         loss = loss + 0.5 * jnp.sum(error * error)
     error_sum = jnp.concatenate(error_sum, axis=1)
@@ -201,7 +202,13 @@
             err[at, :] = unfolded(ag_recv[h, s].astype(jnp.float32))
 
         place_error(me_l)
-        collect(ag_recv.at[h], s4.at[h], r4.at[h], place_error)
+
+        @pl.loop(1, n_l)
+        def _(k):
+            p = lax.rem(me_l + k, n_l)
+            to_latent(ag_recv.at[h, p], ag_recv.at[h, p], s4.at[h], r4.at[h], p, p).wait_recv()
+            place_error(p)
+
         left_ref[count:, cols] = err[...].astype(jnp.bfloat16)
 
         @pl.loop(0, latents // wide)
@@ -247,22 +254,26 @@
         to_latent(vec_l.at[me_l], vec_l.at[me_l], s6, r6, p, me_l).wait_send()
     drain(gathered.at[me_l], gathered, s2, r2)
     for h in range(2):
-        drain(ag_recv.at[h, me_l], ag_recv.at[h], s4.at[h], r4.at[h])
         for p in peers(me_l, n_l):
             to_latent(rs_send.at[h, p], rs_recv.at[h, me_l], s3.at[h], r3.at[h], p, me_l).wait_send()
-
-
-def grad_kernel(left_ref, right_ref, genc_in, gdec_in, loss_in, out_ref, genc_out, gdec_out, loss_out):
-    @pl.when(pl.program_id(0) == 0)
-    def _():
-        genc_out[...] = genc_in[...]
-        gdec_out[...] = gdec_in[...]
-        loss_out[0] = loss_in[0]
-
-    for j in range(right_ref.shape[1] // TILE):
-        at = slice(j * TILE, (j + 1) * TILE)
-        out_ref[0, :, at] = lax.dot_general(
-            left_ref[...], right_ref[:, at], ALONG_FIRST, preferred_element_type=jnp.float32).astype(out_ref.dtype)
+            to_latent(ag_recv.at[h, me_l], ag_recv.at[h, me_l], s4.at[h], r4.at[h], p, me_l).wait_send()
+
+
+def grad_kernel(left_ref, right_ref, genc_in, gdec_in, loss_in, out_ref, genc_out, gdec_out, loss_out, grad, sems):
+    width = grad.shape[0]
+    strip = width // sems.shape[0]
+    copies = []
+    for i in range(sems.shape[0]):
+        at = slice(i * strip, (i + 1) * strip)
+        grad[at, :] = lax.dot_general(
+            left_ref[:, at], right_ref[...], ALONG_FIRST, preferred_element_type=jnp.float32).astype(grad.dtype)
+        copies.append(pltpu.make_async_copy(grad.at[at, :], out_ref.at[0, at, :], sems.at[i]))
+        copies[-1].start()
+    genc_out[...] = genc_in[...]
+    gdec_out[...] = gdec_in[...]
+    loss_out[0] = loss_in[0]
+    for copy in copies:
+        copy.wait()
 
 
 def shards(tokens, route, blocks, weight, enc_bias, dec_bias):
@@ -311,7 +322,7 @@
             dma((n_e,)), dma((n_e,)),
             dma((2 * n_l,)), dma((n_l,)),
             dma((2, n_l)), dma((2, n_l)),
-            dma((2, 2 * n_l)), dma((2, n_l)),
+            dma((2, n_l)), dma((2, n_l)),
             dma((n_e,)), dma((n_e,)),
             dma((n_l,)), dma((n_l,)),
         ],
@@ -319,12 +330,7 @@
             collective_id=0, has_side_effects=True, vmem_limit_bytes=56 << 20),
         name="sae_step",
     )(tokens, route.reshape(1, n_tok), blocks, weight, enc_bias, dec_bias)
-    strip = TILE
-    small = [
-        pl.BlockSpec((1, latents), lambda i: (0, 0)),
-        pl.BlockSpec((width,), lambda i: (0,)),
-        pl.BlockSpec(memory_space=pltpu.SMEM),
-    ]
+    small = [vmem, vmem, pl.BlockSpec(memory_space=pltpu.SMEM)]
     grad, genc, gdec, loss = pl.pallas_call(
         grad_kernel,
         out_shape=(
@@ -333,12 +339,9 @@
             jax.ShapeDtypeStruct((width,), f32),
             jax.ShapeDtypeStruct((1,), f32),
         ),
-        grid=(width // strip,),
-        in_specs=[
-            pl.BlockSpec((2 * count, strip), lambda i: (0, i)),
-            pl.BlockSpec((2 * count, latents), lambda i: (0, 0)),
-        ] + small,
-        out_specs=[pl.BlockSpec((1, strip, latents), lambda i: (0, i, 0))] + small,
+        in_specs=[vmem, vmem] + small,
+        out_specs=[pl.BlockSpec(memory_space=pl.ANY)] + small,
+        scratch_shapes=[pltpu.VMEM((width, latents), bf16), dma((width // TILE,))],
         compiler_params=pltpu.CompilerParams(vmem_limit_bytes=56 << 20),
         name="grad_weight",
     )(left, right, genc, gdec, loss)

time: 61.1 us -> 54.9 us (0.90)
  Pallas kernels: 59.8 us -> 54.1 us
    pallas_call x1, Pallas kernels: 8.76 us -> 5.19 us  [shards(): pl.pallas_call(grad_kernel, out_shape=(jax.ShapeDtypeStruct((1, width, la...]
    pallas_call x1, Pallas kernels: 51.1 us -> 48.9 us  [shards(): pl.pallas_call(functools.partial(step_kernel, n_e, n_l, n_tok, width, lis...]
where the time goes in v4:
time: 54.9 us; the launch traced here: 54.7 us
  Pallas kernels  54.1 us (99%)
  between operations  0.64 us (1%)
    pallas_call x1, Pallas kernels, shards(): pl.pallas_call(functools.partial(step_kernel, n_e, n_l, n_tok, width, lis...  48.9 us
    pallas_call x1, Pallas kernels, shards(): pl.pallas_call(grad_kernel, out_shape=(jax.ShapeDtypeStruct((1, width, la...  5.19 us

profile of v4, /device:TPU:0, one launch (start us, length us, event | category | flops | bytes accessed | tf_op | source)
XLA Modules:
  0.0 54.7 jit_solution(11567134329906600739)
XLA Ops:
  0.6 48.9 %sae_step.1 = (bf16[128,2560]{1,0:T(8,128)(2,1)}, bf16[128,1024]{1,0:T(8,128)(2,1)}, f32[1,1024]{1,0:T(1,128)}, f32[2560]{0:T(1024)}, f32[1]{0:T(128)}) custom-call(bf16[8,2560]{1,0:T(8,128)(2,1)} %tok_ref.1, s32[1,8]{1,0:T(1,128)} %bitcast.2, s32[8,64]{1,0:T(8,128)} %blocks_ref.1, bf16[1,2560,1024]{2,1,0:T(8,128)(2,1)} %w_hbm.1, f32[1,1024]{1,0:T(1,128)} %encb_ref.1, ...), custom_call_target="tpu_custom_call" | custom-call | tf_op jit(solution)/shard_map/sae_step/pallas_call | solution.py:293
  49.5 5.2 %grad_weight.1 = (bf16[1,2560,1024]{2,1,0:T(8,128)(2,1)}, f32[1,1024]{1,0:T(1,128)}, f32[2560]{0:T(1024)}, f32[1]{0:T(128)}) custom-call(bf16[128,2560]{1,0:T(8,128)(2,1)} %get-tuple-element.13.left_ref, bf16[128,1024]{1,0:T(8,128)(2,1)} %get-tuple-element.14.right_ref, f32[1,1024]{1,0:T(1,128)} %get-tuple-element.15.genc_in, ...), custom_call_target="tpu_custom_call" | custom-call | tf_op jit(solution)/shard_map/grad_weight/pallas_call | solution.py:334

commit v5 on v4

--- a/solution.py
+++ b/solution.py
@@ -20,9 +20,9 @@
 def step_kernel(
     n_e, n_l, n_tok, width, list_len,
     tok_ref, route_ref, blocks_ref, w_hbm, encb_ref, decb_ref,
-    left_ref, right_ref, genc_ref, gdec_ref, loss_ref,
-    w_ref, aug, pack, mine, gathered, rows, shifted, gate, part, rs_send, rs_recv, ag_recv, err, acc, vec_e, vec_l,
-    w_sem, s1, r1, s2, r2, s3, r3, s4, r4, s5, r5, s6, r6,
+    left_out, right_out, genc_ref, gdec_ref, loss_ref,
+    left_ref, right_ref, w_ref, aug, pack, mine, gathered, rows, shifted, gate, part, rs_send, rs_recv, ag_recv, err, acc, vec_e, vec_l,
+    w_sem, out_sem, s1, r1, s2, r2, s3, r3, s4, r4, s5, r5, s6, r6,
 ):
     me_e = lax.axis_index("expert")
     me_l = lax.axis_index("latent")
@@ -46,6 +46,11 @@
             src_ref=src, dst_ref=dst, send_sem=ssem.at[peer], recv_sem=rsem.at[slot],
             device_id=(me_e, peer), device_id_type=MESH)
 
+    def steps(n):
+        if n == 1:
+            return lambda body: body(0)
+        return pl.loop(0, n)
+
     def peers(me, n):
         return [lax.rem(me + k, n) for k in range(1, n)]
 
@@ -80,13 +85,14 @@
                 src_ref=dst.at[p], dst_ref=dst.at[p], send_sem=ssem.at[n_l + p], recv_sem=rsem.at[p],
                 device_id=(me_e, partner), device_id_type=MESH).wait_send()
 
-    w_copy = pltpu.make_async_copy(w_hbm.at[0], w_ref, w_sem)
-    w_copy.start()
     barrier = pltpu.get_barrier_semaphore()
     for p in peers(me_e, n_e):
         pl.semaphore_signal(barrier, inc=1, device_id=(p, me_l), device_id_type=MESH)
     for p in peers(me_l, n_l):
         pl.semaphore_signal(barrier, inc=1, device_id=(me_e, p), device_id_type=MESH)
+
+    w_copy = pltpu.make_async_copy(w_hbm.at[0], w_ref, w_sem)
+    w_copy.start()
 
     aug[...] = jnp.zeros_like(aug)
     aug[:, :width] = tok_ref[...].astype(jnp.float32)
@@ -147,9 +153,9 @@
 
     w_copy.wait()
 
-    @pl.loop(0, latents // wide)
+    @steps(latents // wide)
     def _(j):
-        at = pl.ds(pl.multiple_of(j * wide, wide), wide)
+        at = pl.ds(j * wide if few else pl.multiple_of(j * wide, wide), wide)
         pre = jnp.dot(shifted[...], w_ref[:, at], preferred_element_type=jnp.float32) + encb_ref[:, at]
         mask = gate[:, at]
         right_ref[count:, at] = (jnp.maximum(pre, 0.0) * mask).astype(jnp.bfloat16)
@@ -163,9 +169,9 @@
 
     own = pl.ds(pl.multiple_of(me_l * share, 8), share)
     for h in range(2):
-        @pl.loop(0, half // deep)
+        @steps(half // deep)
         def _(j):
-            at = pl.ds(pl.multiple_of(h * half + j * deep, deep), deep)
+            at = pl.ds(h * half + j * deep if few else pl.multiple_of(h * half + j * deep, deep), deep)
             part[:, at] = lax.dot_general(
                 right_ref[count:, :], w_ref[at, :], ALONG_LAST, preferred_element_type=jnp.float32)
 
@@ -211,9 +217,9 @@
 
         left_ref[count:, cols] = err[...].astype(jnp.bfloat16)
 
-        @pl.loop(0, latents // wide)
+        @steps(latents // wide)
         def _(j):
-            at = pl.ds(pl.multiple_of(j * wide, wide), wide)
+            at = pl.ds(j * wide if few else pl.multiple_of(j * wide, wide), wide)
             grad = jnp.dot(left_ref[count:, cols], w_ref[cols, at], preferred_element_type=jnp.float32)
             if h == 0:
                 acc[:, at] = grad
@@ -222,40 +228,51 @@
                 right_ref[:count, at] = grad.astype(jnp.bfloat16)
                 genc_ref[:, at] = jnp.sum(grad, axis=0, keepdims=True)
 
+    stores = [pltpu.make_async_copy(left_ref, left_out, out_sem.at[0]),
+              pltpu.make_async_copy(right_ref, right_out, out_sem.at[1])]
+    for copy in stores:
+        copy.start()
+
     column = jnp.broadcast_to(genc_ref[...], (8, latents)).astype(jnp.bfloat16)
-    for j in range(width // TILE):
-        at = slice(j * TILE, (j + 1) * TILE)
-        pulled = lax.dot_general(column, w_ref[at, :], ALONG_LAST, preferred_element_type=jnp.float32)
-        vec_e[me_e, :, at] = error_sum[:, at] - pulled[:1]
-    vec_e[me_e, :, width:] = jnp.broadcast_to(loss.reshape(1, 1), (1, LANES))
-
-    for p in peers(me_e, n_e):
-        to_expert(vec_e.at[me_e], vec_e.at[me_e], s5, r5, p, me_e).start()
-    for p in peers(me_e, n_e):
-        to_expert(vec_e.at[p], vec_e.at[p], s5, r5, p, p).wait_recv()
-    vec = vec_e[0]
-    for s in range(1, n_e):
-        vec = vec + vec_e[s]
-    vec_l[me_l] = vec
-    for p in peers(me_l, n_l):
-        to_latent(vec_l.at[me_l], vec_l.at[me_l], s6, r6, p, me_l).start()
-    for p in peers(me_l, n_l):
-        to_latent(vec_l.at[p], vec_l.at[p], s6, r6, p, p).wait_recv()
-    vec = vec_l[0]
-    for s in range(1, n_l):
-        vec = vec + vec_l[s]
-    gdec_ref[...] = vec[:, :width].reshape(width)
-    loss_ref[0] = vec[0, width] * (1.0 / (n_tok * n_e * n_l))
+    for h in range(2):
+        for j in range(half // TILE):
+            at = slice(h * half + j * TILE, h * half + (j + 1) * TILE)
+            pulled = lax.dot_general(column, w_ref[at, :], ALONG_LAST, preferred_element_type=jnp.float32)
+            vec_e[h, me_e, :, j * TILE:(j + 1) * TILE] = error_sum[:, at] - pulled[:1]
+        vec_e[h, me_e, :, half:] = jnp.broadcast_to(loss.reshape(1, 1), (1, LANES))
+        for p in peers(me_e, n_e):
+            to_expert(vec_e.at[h, me_e], vec_e.at[h, me_e], s5.at[h], r5.at[h], p, me_e).start()
+    for h in range(2):
+        for p in peers(me_e, n_e):
+            to_expert(vec_e.at[h, p], vec_e.at[h, p], s5.at[h], r5.at[h], p, p).wait_recv()
+        vec = vec_e[h, 0]
+        for s in range(1, n_e):
+            vec = vec + vec_e[h, s]
+        vec_l[h, me_l] = vec
+        for p in peers(me_l, n_l):
+            to_latent(vec_l.at[h, me_l], vec_l.at[h, me_l], s6.at[h], r6.at[h], p, me_l).start()
+    ends = []
+    for h in range(2):
+        for p in peers(me_l, n_l):
+            to_latent(vec_l.at[h, p], vec_l.at[h, p], s6.at[h], r6.at[h], p, p).wait_recv()
+        vec = vec_l[h, 0]
+        for s in range(1, n_l):
+            vec = vec + vec_l[h, s]
+        ends.append(vec)
+    gdec_ref[...] = jnp.concatenate([ends[0][:, :half], ends[1][:, :half]], axis=1).reshape(width)
+    loss_ref[0] = ends[0][0, half] * (1.0 / (n_tok * n_e * n_l))
+    for copy in stores:
+        copy.wait()
 
     for p in peers(me_e, n_e):
         to_expert(pack.at[p], mine.at[me_e], s1, r1, p, me_e).wait_send()
-        to_expert(vec_e.at[me_e], vec_e.at[me_e], s5, r5, p, me_e).wait_send()
-    for p in peers(me_l, n_l):
-        to_latent(vec_l.at[me_l], vec_l.at[me_l], s6, r6, p, me_l).wait_send()
+        for h in range(2):
+            to_expert(vec_e.at[h, me_e], vec_e.at[h, me_e], s5.at[h], r5.at[h], p, me_e).wait_send()
     drain(gathered.at[me_l], gathered, s2, r2)
     for h in range(2):
         for p in peers(me_l, n_l):
             to_latent(rs_send.at[h, p], rs_recv.at[h, me_l], s3.at[h], r3.at[h], p, me_l).wait_send()
+            to_latent(vec_l.at[h, me_l], vec_l.at[h, me_l], s6.at[h], r6.at[h], p, me_l).wait_send()
             to_latent(ag_recv.at[h, me_l], ag_recv.at[h, me_l], s4.at[h], r4.at[h], p, me_l).wait_send()
 
 
@@ -300,8 +317,10 @@
             jax.ShapeDtypeStruct((1,), f32),
         ),
         in_specs=[vmem, vmem, vmem, pl.BlockSpec(memory_space=pl.ANY), vmem, vmem],
-        out_specs=[vmem] * 4 + [pl.BlockSpec(memory_space=pltpu.SMEM)],
+        out_specs=[pl.BlockSpec(memory_space=pl.ANY)] * 2 + [vmem] * 2 + [pl.BlockSpec(memory_space=pltpu.SMEM)],
         scratch_shapes=[
+            pltpu.VMEM((2 * count, width), bf16),
+            pltpu.VMEM((2 * count, latents), bf16),
             pltpu.VMEM((width, latents), bf16),
             pltpu.VMEM((n_tok, aug_width), f32),
             pltpu.VMEM((n_e, PACK, chunk), bf16),
@@ -316,15 +335,15 @@
             pltpu.VMEM((2, n_l, 2 * share, width // 4), bf16),
             pltpu.VMEM((count, width // 2), f32),
             pltpu.VMEM((count, latents), f32),
-            pltpu.VMEM((n_e, 1, width + LANES), f32),
-            pltpu.VMEM((n_l, 1, width + LANES), f32),
-            dma,
+            pltpu.VMEM((2, n_e, 1, width // 2 + LANES), f32),
+            pltpu.VMEM((2, n_l, 1, width // 2 + LANES), f32),
+            dma, dma((2,)),
             dma((n_e,)), dma((n_e,)),
             dma((2 * n_l,)), dma((n_l,)),
             dma((2, n_l)), dma((2, n_l)),
             dma((2, n_l)), dma((2, n_l)),
-            dma((n_e,)), dma((n_e,)),
-            dma((n_l,)), dma((n_l,)),
+            dma((2, n_e)), dma((2, n_e)),
+            dma((2, n_l)), dma((2, n_l)),
         ],
         compiler_params=pltpu.CompilerParams(
             collective_id=0, has_side_effects=True, vmem_limit_bytes=56 << 20),

time: 54.9 us -> 54.7 us (level)
  no operation moved by 1% of the time
where the time goes in v5:
time: 54.7 us; the launch traced here: 54.5 us
  Pallas kernels  53.8 us (98%)
  between operations  0.64 us (1%)
    pallas_call x1, Pallas kernels, shards(): pl.pallas_call(functools.partial(step_kernel, n_e, n_l, n_tok, width, lis...  48.7 us
    pallas_call x1, Pallas kernels, shards(): pl.pallas_call(grad_kernel, out_shape=(jax.ShapeDtypeStruct((1, width, la...  5.19 us

profile of v5, /device:TPU:0, one launch (start us, length us, event | category | flops | bytes accessed | tf_op | source)
XLA Modules:
  0.0 54.5 jit_solution(16070765678468247208)
XLA Ops:
  0.6 48.7 %sae_step.1 = (bf16[128,2560]{1,0:T(8,128)(2,1)}, bf16[128,1024]{1,0:T(8,128)(2,1)}, f32[1,1024]{1,0:T(1,128)}, f32[2560]{0:T(1024)}, f32[1]{0:T(128)}) custom-call(bf16[8,2560]{1,0:T(8,128)(2,1)} %tok_ref.1, s32[1,8]{1,0:T(1,128)} %bitcast.2, s32[8,64]{1,0:T(8,128)} %blocks_ref.1, bf16[1,2560,1024]{2,1,0:T(8,128)(2,1)} %w_hbm.1, f32[1,1024]{1,0:T(1,128)} %encb_ref.1, ...), custom_call_target="tpu_custom_call" | custom-call | tf_op jit(solution)/shard_map/sae_step/pallas_call | solution.py:310
  49.3 5.2 %grad_weight.1 = (bf16[1,2560,1024]{2,1,0:T(8,128)(2,1)}, f32[1,1024]{1,0:T(1,128)}, f32[2560]{0:T(1024)}, f32[1]{0:T(128)}) custom-call(bf16[128,2560]{1,0:T(8,128)(2,1)} %get-tuple-element.13.left_ref, bf16[128,1024]{1,0:T(8,128)(2,1)} %get-tuple-element.14.right_ref, f32[1,1024]{1,0:T(1,128)} %get-tuple-element.15.genc_in, ...), custom_call_target="tpu_custom_call" | custom-call | tf_op jit(solution)/shard_map/grad_weight/pallas_call | solution.py:353

commit v6 on v5

--- a/solution.py
+++ b/solution.py
@@ -53,37 +53,6 @@
 
     def peers(me, n):
         return [lax.rem(me + k, n) for k in range(1, n)]
-
-    partner = me_l + 1 - 2 * lax.rem(me_l, 2)
-    alike = [lax.rem(me_l + 2 * k, n_l) for k in range(1, n_l // 2)]
-
-    def spread(src, dst, ssem, rsem):
-        for p in alike + [partner]:
-            to_latent(src, dst.at[me_l], ssem, rsem, p, me_l).start()
-
-    def collect(dst, ssem, rsem, use):
-        @pl.loop(1, n_l // 2)
-        def _(k):
-            p = lax.rem(me_l + 2 * k, n_l)
-            to_latent(dst.at[p], dst.at[p], ssem, rsem, p, p).wait_recv()
-            pltpu.make_async_remote_copy(
-                src_ref=dst.at[p], dst_ref=dst.at[p], send_sem=ssem.at[n_l + p], recv_sem=rsem.at[p],
-                device_id=(me_e, partner), device_id_type=MESH).start()
-            use(p)
-
-        @pl.loop(0, n_l // 2)
-        def _(k):
-            p = lax.rem(partner + 2 * k, n_l)
-            to_latent(dst.at[p], dst.at[p], ssem, rsem, p, p).wait_recv()
-            use(p)
-
-    def drain(src, dst, ssem, rsem):
-        for p in alike + [partner]:
-            to_latent(src, dst.at[me_l], ssem, rsem, p, me_l).wait_send()
-        for p in alike:
-            pltpu.make_async_remote_copy(
-                src_ref=dst.at[p], dst_ref=dst.at[p], send_sem=ssem.at[n_l + p], recv_sem=rsem.at[p],
-                device_id=(me_e, partner), device_id_type=MESH).wait_send()
 
     barrier = pltpu.get_barrier_semaphore()
     for p in peers(me_e, n_e):
@@ -129,7 +98,8 @@
     flat = jnp.concatenate([flat[c * share:(c + 1) * share] for c in range(PARTS)], axis=1)
     fold = gathered.shape[2]
     gathered[me_l] = jnp.concatenate([flat[:, :fold], flat[:, fold:2 * fold]], axis=0).astype(jnp.bfloat16)
-    spread(gathered.at[me_l], gathered, s2, r2)
+    for p in peers(me_l, n_l):
+        to_latent(gathered.at[me_l], gathered.at[me_l], s2, r2, p, me_l).start()
 
     def place_rows(source):
         block = gathered[source].astype(jnp.float32)
@@ -138,7 +108,12 @@
         rows[at, fold:] = block[share:]
 
     place_rows(me_l)
-    collect(gathered, s2, r2, place_rows)
+
+    @pl.loop(1, n_l)
+    def _(k):
+        p = lax.rem(me_l + k, n_l)
+        to_latent(gathered.at[p], gathered.at[p], s2, r2, p, p).wait_recv()
+        place_rows(p)
 
     decb = decb_ref[...].reshape(1, width)
     bf = (rows[:, :width] - decb).astype(jnp.bfloat16)
@@ -268,7 +243,8 @@
         to_expert(pack.at[p], mine.at[me_e], s1, r1, p, me_e).wait_send()
         for h in range(2):
             to_expert(vec_e.at[h, me_e], vec_e.at[h, me_e], s5.at[h], r5.at[h], p, me_e).wait_send()
-    drain(gathered.at[me_l], gathered, s2, r2)
+    for p in peers(me_l, n_l):
+        to_latent(gathered.at[me_l], gathered.at[me_l], s2, r2, p, me_l).wait_send()
     for h in range(2):
         for p in peers(me_l, n_l):
             to_latent(rs_send.at[h, p], rs_recv.at[h, me_l], s3.at[h], r3.at[h], p, me_l).wait_send()
@@ -339,7 +315,7 @@
             pltpu.VMEM((2, n_l, 1, width // 2 + LANES), f32),
             dma, dma((2,)),
             dma((n_e,)), dma((n_e,)),
-            dma((2 * n_l,)), dma((n_l,)),
+            dma((n_l,)), dma((n_l,)),
             dma((2, n_l)), dma((2, n_l)),
             dma((2, n_l)), dma((2, n_l)),
             dma((2, n_e)), dma((2, n_e)),

time: 54.7 us -> 54.9 us (level)
  no operation moved by 1% of the time
where the time goes in v6:
time: 54.9 us; the launch traced here: 54.7 us
  Pallas kernels  54.1 us (99%)
  between operations  0.64 us (1%)
    pallas_call x1, Pallas kernels, shards(): pl.pallas_call(functools.partial(step_kernel, n_e, n_l, n_tok, width, lis...  48.9 us
    pallas_call x1, Pallas kernels, shards(): pl.pallas_call(grad_kernel, out_shape=(jax.ShapeDtypeStruct((1, width, la...  5.19 us

profile of v6, /device:TPU:0, one launch (start us, length us, event | category | flops | bytes accessed | tf_op | source)
XLA Modules:
  0.0 54.7 jit_solution(5694938665043101031)
XLA Ops:
  0.6 48.9 %sae_step.1 = (bf16[128,2560]{1,0:T(8,128)(2,1)}, bf16[128,1024]{1,0:T(8,128)(2,1)}, f32[1,1024]{1,0:T(1,128)}, f32[2560]{0:T(1024)}, f32[1]{0:T(128)}) custom-call(bf16[8,2560]{1,0:T(8,128)(2,1)} %tok_ref.1, s32[1,8]{1,0:T(1,128)} %bitcast.2, s32[8,64]{1,0:T(8,128)} %blocks_ref.1, bf16[1,2560,1024]{2,1,0:T(8,128)(2,1)} %w_hbm.1, f32[1,1024]{1,0:T(1,128)} %encb_ref.1, ...), custom_call_target="tpu_custom_call" | custom-call | tf_op jit(solution)/shard_map/sae_step/pallas_call | solution.py:286
  49.5 5.2 %grad_weight.1 = (bf16[1,2560,1024]{2,1,0:T(8,128)(2,1)}, f32[1,1024]{1,0:T(1,128)}, f32[2560]{0:T(1024)}, f32[1]{0:T(128)}) custom-call(bf16[128,2560]{1,0:T(8,128)(2,1)} %get-tuple-element.13.left_ref, bf16[128,1024]{1,0:T(8,128)(2,1)} %get-tuple-element.14.right_ref, f32[1,1024]{1,0:T(1,128)} %get-tuple-element.15.genc_in, ...), custom_call_target="tpu_custom_call" | custom-call | tf_op jit(solution)/shard_map/grad_weight/pallas_call | solution.py:329
